TPU v7x, 512 devices: a whole 4x4x16 slice. The times are simulated.
512 devices in a mesh: tm: 16 (over z), query: 8 (over y, core), rec: 4 (over x).
Axes of the slice: x: 4, y: 4, z: 16, core: 2. Of those that a mesh axis runs over, the one named last changes fastest.
Arguments:
- frames: bfloat16 [4, 8192, 1024], P('rec', 'tm'), may hold values from -100 to 100
- queries: bfloat16 [4096, 1024], P('query'), may hold values from -10 to 10
- kernel: float32 [33, 4096], P(None, 'query'), may hold values from 0.01 to 0.12
- labels: int32 [4, 8192], P('rec', 'tm'), may hold values from 0 to 4095
- lengths: int32 [4], P('rec'), may hold values from 2048 to 8192, as said below
Outputs:
- grad_frames: bfloat16 [4, 8192, 1024], P('rec', 'tm', 'query')
- grad_queries: bfloat16 [4096, 1024], P('query', 'rec')
- grad_kernel: float32 [33, 4096], P(None, 'query')
Inputs may be any that keep to these rules, and one draw needn't show every extreme that they name: `lengths`: each entry counts the valid frames at the start of its recording; at least one recording has all 8192 frames valid.
All inputs are finite; a program needn't handle non-finite values.
Results may differ from a plain program's by a relative error of at most 0.0049.
Values sent between devices are 32-bit elements; how exact they have to be, the bound alone decides.
No kernel may reach another device: no remote copies, remote signals or barrier semaphores. Data moves between devices by JAX's collectives and lax.ppermute only.
A program may use at most 64 MiB of HBM per device.

v0:
```python
import math
import jax
import jax.numpy as jnp
from jax import lax
from jax.sharding import PartitionSpec as P


def merged(x, axis, combine):
    everything = jax.tree.map(lambda part: lax.all_gather(part, axis), x)
    first = jax.tree.map(lambda part: part[0], everything)

    def step(k, so_far):
        return combine(so_far, jax.tree.map(lambda part: part[k], everything))

    return lax.fori_loop(1, lax.axis_size(axis), step, first)


def with_halo(x, sides, width):
    for axis, dim in sides:
        peers, length = (lax.axis_size(axis), x.shape[dim])
        up = [(i, (i + 1) % peers) for i in range(peers - 1)]
        down = [(j, i) for i, j in up]
        last = lax.slice_in_dim(x, length - width, length, axis=dim)
        first = lax.slice_in_dim(x, 0, width, axis=dim)
        before = lax.ppermute(last, axis, up)
        after = lax.ppermute(first, axis, down)
        x = jnp.concatenate([before, x, after], axis=dim)
    return x


def tap_sum(kernel, padded, row_count, flipped):
    tap_count = kernel.shape[0]
    running = jnp.zeros((row_count, padded.shape[1]), jnp.float32)
    for offset in range(tap_count):
        begin_row = tap_count - 1 - offset if flipped else offset
        running = running + kernel[offset][None, :] * padded[begin_row : begin_row + row_count]
    return running


def combine_stats(first_pair, second_pair):
    top_value = jnp.maximum(first_pair[0], second_pair[0])
    total_value = first_pair[1] * jnp.exp(first_pair[0] - top_value) + second_pair[1] * jnp.exp(
        second_pair[0] - top_value
    )
    return (top_value, total_value)


def row_softmax(smooth):
    local_top = jnp.max(smooth, axis=1)
    local_total = jnp.sum(jnp.exp(smooth - local_top[:, None]), axis=1)
    top_value, total_value = merged((local_top, local_total), "query", combine_stats)
    return jnp.exp(smooth - top_value[:, None]) / total_value[:, None]


def per_device(frames, queries, kernel, labels, lengths):
    frame_rows = frames[0]
    label_ids = labels[0]
    length_now = lengths[0]
    row_count = frame_rows.shape[0]
    query_count = queries.shape[0]
    width = frame_rows.shape[1]
    tap_count = kernel.shape[0]
    rim_width = tap_count // 2
    logit_scale = 10.0 / math.sqrt(width)
    frame_start = lax.axis_index("tm") * row_count
    is_valid = frame_start + jnp.arange(row_count, dtype=jnp.int32) < length_now
    query_start = lax.axis_index("query") * query_count
    query_ids = query_start + jnp.arange(query_count, dtype=jnp.int32)
    scores = (
        lax.dot_general(
            frame_rows, queries, (((1,), (1,)), ((), ())), preferred_element_type=jnp.float32
        )
        * logit_scale
    )
    scores = jnp.where(is_valid[:, None], scores, 0.0)
    padded = with_halo(scores, (("tm", 0),), rim_width)
    smooth = tap_sum(kernel, padded, row_count, False)
    softmax_out = row_softmax(smooth)
    positive = (label_ids[:, None] == query_ids[None, :]).astype(jnp.float32)
    map_grad = jnp.where(is_valid[:, None], softmax_out - positive, 0.0)
    grad_pad = with_halo(map_grad, (("tm", 0),), rim_width)
    score_grad = tap_sum(kernel, grad_pad, row_count, True)
    score_grad = jnp.where(is_valid[:, None], score_grad, 0.0).astype(jnp.bfloat16)
    frame_part = jnp.dot(score_grad, queries, preferred_element_type=jnp.float32)
    frame_sum = lax.psum_scatter(frame_part, "query", scatter_dimension=1, tiled=True)
    grad_frames = (frame_sum * logit_scale).astype(jnp.bfloat16)[None]
    query_part = lax.dot_general(
        score_grad, frame_rows, (((0,), (0,)), ((), ())), preferred_element_type=jnp.float32
    )
    kernel_part = jnp.stack(
        [
            jnp.sum(map_grad * padded[offset : offset + row_count], axis=0)
            for offset in range(tap_count)
        ]
    )
    query_whole, grad_kernel = lax.psum((query_part, kernel_part), ("tm", "rec"))
    col_count = width // lax.axis_size("rec")
    query_cols = lax.dynamic_slice_in_dim(
        query_whole, lax.axis_index("rec") * col_count, col_count, 1
    )
    grad_queries = (query_cols * logit_scale).astype(jnp.bfloat16)
    return (grad_frames, grad_queries, grad_kernel)


def solution(mesh):
    in_specs = (P("rec", "tm", None), P("query", None), P(None, "query"), P("rec", "tm"), P("rec"))
    out_specs = (P("rec", "tm", "query"), P("query", "rec"), P(None, "query"))
    return jax.shard_map(
        per_device, mesh=mesh, in_specs=in_specs, out_specs=out_specs, check_vma=False
    )
```

profile of v0, /device:TPU:8, one launch (start us, length us, event | category | flops | bytes accessed | tf_op | source)
XLA Modules:
  0.0 376.1 jit_solution(3690222084819182365)
XLA Ops:
  8.0 0.0 copy-start
  8.0 0.0 all-reduce.3.cloned.1.call-start
  8.8 0.4 copy-done
  9.2 2.0 fusion
  11.3 3.8 %collective-permute-start = (f32[16,512]{1,0:T(8,128)S(1)}, f32[16,512]{1,0:T(8,128)S(1)}, u32[]{:S(2)}, u32[]{:S(2)}) collective-permute-start(f32[16,512]{1,0:T(8,128)S(1)} %get-tuple-element.192), channel_id=1, source_target_pairs={{0,32},{32,64},{64,96},{96,128},{128,160},{160,192},{192,224},{224... | collective-permute-start | bytes 98312 | tf_op jit(solution)/shard_map/ppermute | solution.py:25
  15.1 1.3 collective-permute-start.1
  16.5 0.2 collective-permute-done
  16.7 4.2 %collective-permute-done.1 = f32[16,512]{1,0:T(8,128)S(1)} collective-permute-done((f32[16,512]{1,0:T(8,128)S(1)}, f32[16,512]{1,0:T(8,128)S(1)}, u32[]{:S(2)}, u32[]{:S(2)}) %collective-permute-start.1) | collective-permute-done | bytes 32800 | tf_op jit(solution)/shard_map/ppermute | solution.py:26
  20.9 5.1 %fusion.131 = (f32[512]{0:T(512)S(1)}, f32[512,512]{1,0:T(8,128)S(1)}) fusion(f32[16,512]{1,0:T(8,128)S(1)} %collective-permute-done.1, f32[512,512]{1,0:T(8,128)S(1)} %fusion, f32[512]{0:T(512)S(1)} %bitcast.126, f32[512]{0:T(512)S(1)} %bitcast.128, f32[512]{0:T(512)S(1)} %bitcast.132, f32[512]{0:T(512)S(1)} %bitcast.134, f32[512]{0:T(512)S(1)} %bitcast.136, ...), kind=kLoop, calls=%fused_computation.265 | loop fusion | flops 25689600 | bytes 2232320 | tf_op jit(solution)/shard_map/reduce_max | solution.py:49
  26.1 1.0 copy-done.1
  27.0 0.3 exponential_reduce_fusion
  27.3 12.2 %all-gather.3 = f32[8,1,512]{2,1,0:T(1,128)S(1)} all-gather(f32[1,1,512]{2,1,0:T(1,128)S(1)} %bitcast.194), channel_id=3, replica_groups=mesh['tm'=16,'query'=8,'rec'=4] {'query'}, dimensions={0}, use_global_device_ids=true | all-gather | bytes 18432 | tf_op jit(solution)/shard_map/all_gather | solution.py:9
  39.5 12.0 %all-gather.2 = f32[8,1,512]{2,1,0:T(1,128)S(1)} all-gather(f32[1,1,512]{2,1,0:T(1,128)S(1)} %bitcast.168), channel_id=2, replica_groups=mesh['tm'=16,'query'=8,'rec'=4] {'query'}, dimensions={0}, use_global_device_ids=true | all-gather | bytes 18432 | tf_op jit(solution)/shard_map/all_gather | solution.py:9
  51.4 0.4 while.17
  51.8 4.3 %multiply_reduce_fusion = (f32[512]{0:T(512)S(1)}, f32[512]{0:T(512)S(1)}, f32[512]{0:T(512)S(1)}, f32[512]{0:T(512)S(1)}, f32[512]{0:T(512)S(1)}, /*index=5*/f3...) fusion(f32[16,512]{1,0:T(8,128)S(1)} %collective-permute-done.1, ...), kind=kLoop, calls=%fused_computation.222 | loop fusion | flops 8646144 | bytes 3205632 | tf_op jit(solution)/shard_map/reduce_sum | solution.py:92
  56.1 1.3 collective-permute-start.2
  57.4 4.5 %collective-permute-start.3 = (f32[16,512]{1,0:T(8,128)S(1)}, f32[16,512]{1,0:T(8,128)S(1)}, u32[]{:S(2)}, u32[]{:S(2)}) collective-permute-start(f32[16,512]{1,0:T(8,128)S(1)} %get-tuple-element.191), channel_id=1, source_target_pairs={{0,32},{32,64},{64,96},{96,128},{128,160},{160,192},{192,224},{224... | collective-permute-start | bytes 98312 | tf_op jit(solution)/shard_map/ppermute | solution.py:25
  62.0 1.9 multiply_reduce_fusion.1
  63.9 1.2 multiply_reduce_fusion.17
  65.1 1.0 multiply_reduce_fusion.26
  66.1 3.9 %stack.135 = f32[33,512]{1,0:T(8,128)} concatenate(f32[1,512]{1,0:T(1,128)S(1)} %bitcast.193, f32[1,512]{1,0:T(1,128)S(1)} %bitcast.192, f32[1,512]{1,0:T(1,128)S(1)} %bitcast.191, f32[1,512]{1,0:T(1,128)S(1)} %bitcast.190, f32[1,512]{1,0:T(1,128)S(1)} %bitcast.189, f32[1,512]{1,0:T(1,128)S(1)} %bitcast.188, f32[1,512]{1,0:T(1,128)S(1)} %bitcast.187, f32[1,512]{1,0:T(1,128)S(1)} %bitcast.186, ...), dimensions={0} | concatenate | bytes 135168 | tf_op jit(solution)/shard_map/stack | solution.py:90
  70.0 8.6 %fusion.6 = bf16[512,512]{1,0:T(8,128)(2,1)S(1)} fusion(f32[16,512]{1,0:T(8,128)S(1)} %collective-permute-done.3, f32[16,512]{1,0:T(8,128)S(1)} %collective-permute-done.2, f32[512,512]{1,0:T(8,128)S(1)} %get-tuple-element.185, f32[512]{0:T(512)S(1)} %bitcast.127, f32[512]{0:T(512)S(1)} %bitcast.129, f32[512]{0:T(512)S(1)} %bitcast.133, ...), kind=kLoop, calls=%fused_computation.70 | loop fusion | flops 25952256 | bytes 1706496 | tf_op jit(solution)/shard_map/convert_element_type | solution.py:83
  78.5 2.0 fusion.127
  80.6 0.0 all-reduce.3.cloned.1.call-update
  80.6 0.0 reduce-scatter.2.cloned.1.call-start
  80.7 1.1 copy-done.2
  81.8 2.0 fusion.136
  83.9 0.0 reduce-scatter.2.cloned.1.call-update
  83.9 280.7 %all-reduce.3.cloned.1.call-done = (f32[512,1024]{1,0:T(8,128)}, f32[33,512]{1,0:T(8,128)}) async-done(((f32[512,1024]{1,0:T(8,128)}, f32[33,512]{1,0:T(8,128)}), (f32[512,1024]{1,0:T(8,128)}, f32[33,512]{1,0:T(8,128)})) %all-reduce.3.cloned.1.call-update) | async-done | bytes 2164752 | tf_op jit(solution)/shard_map/psum | solution.py:96
  364.6 1.8 multiply_convert_fusion
  366.4 1.6 fusion.130
  368.1 0.6 copy.26
  (37 shorter events, 0.3 us)
Async XLA Ops:
  8.0 1.2 copy-start
  8.0 356.6 %all-reduce.3.cloned.1.call-start = ((), (), s32[]{:S(2)}) async-start(), calls=%async_computation.2 | async-start | bytes 4358144 | tf_op jit(solution)/shard_map/psum | solution.py:96
  9.2 42.6 %copy-start.5 = (pred[512]{0:T(512)(128)(4,1)}, pred[512]{0:T(512)(128)(4,1)S(1)}, u32[]{:S(2)}) copy-start(pred[512]{0:T(512)(128)(4,1)S(1)} %add_compare_fusion) | copy-start | bytes 1540
  9.2 7.2 %copy-start.4 = (f32[33,512]{1,0:T(8,128)S(1)}, f32[33,512]{1,0:T(8,128)}, u32[]{:S(2)}) copy-start(f32[33,512]{1,0:T(8,128)} %param.9) | copy-start | bytes 202756
  11.3 5.4 %collective-permute-start = (f32[16,512]{1,0:T(8,128)S(1)}, f32[16,512]{1,0:T(8,128)S(1)}, u32[]{:S(2)}, u32[]{:S(2)}) collective-permute-start(f32[16,512]{1,0:T(8,128)S(1)} %get-tuple-element.192), channel_id=1, source_target_pairs={{0,32},{32,64},{64,96},{96,128},{128,160},{160,192},{192,224},{224... | collective-permute-start | bytes 98312 | tf_op jit(solution)/shard_map/ppermute | solution.py:25
  15.1 5.8 %collective-permute-start.1 = (f32[16,512]{1,0:T(8,128)S(1)}, f32[16,512]{1,0:T(8,128)S(1)}, u32[]{:S(2)}, u32[]{:S(2)}) collective-permute-start(f32[16,512]{1,0:T(8,128)S(1)} %get-tuple-element.193), channel_id=1, source_target_pairs={{32,0},{64,32},{96,64},{128,96},{160,128},{192,160},{224,192},{256... | collective-permute-start | bytes 98312 | tf_op jit(solution)/shard_map/ppermute | solution.py:26
  26.0 1.0 copy-start.1
  26.0 25.8 %copy-start.6 = (s32[1,512]{1,0:T(1,128)S(1)}, s32[1,512]{1,0:T(1,128)}, u32[]{:S(2)}) copy-start(s32[1,512]{1,0:T(1,128)} %param.10) | copy-start | bytes 6148
  56.1 13.9 %collective-permute-start.2 = (f32[16,512]{1,0:T(8,128)S(1)}, f32[16,512]{1,0:T(8,128)S(1)}, u32[]{:S(2)}, u32[]{:S(2)}) collective-permute-start(f32[16,512]{1,0:T(8,128)S(1)} %get-tuple-element.190), channel_id=1, source_target_pairs={{32,0},{64,32},{96,64},{128,96},{160,128},{192,160},{224,192},{256... | collective-permute-start | bytes 98312 | tf_op jit(solution)/shard_map/ppermute | solution.py:26
  57.4 12.6 %collective-permute-start.3 = (f32[16,512]{1,0:T(8,128)S(1)}, f32[16,512]{1,0:T(8,128)S(1)}, u32[]{:S(2)}, u32[]{:S(2)}) collective-permute-start(f32[16,512]{1,0:T(8,128)S(1)} %get-tuple-element.191), channel_id=1, source_target_pairs={{0,32},{32,64},{64,96},{96,128},{128,160},{160,192},{192,224},{224... | collective-permute-start | bytes 98312 | tf_op jit(solution)/shard_map/ppermute | solution.py:25
  80.6 1.2 copy-start.2
  80.6 285.8 %reduce-scatter.2.cloned.1.call-start = ((), (), s32[]{:S(2)}) async-start(), calls=%async_computation.1 | async-start | bytes 2359296 | tf_op jit(solution)/shard_map/reduce_scatter | solution.py:85
  364.6 3.4 copy-start.3
Sparse Core Ops, SparseCore 0:
  80.7 283.8 all-reduce.2
Sparse Core Ops, SparseCore 1:
  84.0 42.4 reduce-scatter.1
where the time goes:
time: 377 us; the launch traced here: 376 us
  waiting for transfers between devices  285 us (76%)
  other arithmetic  25.9 us (7%)
  blocking collectives  24.1 us (6%)
  between operations  16.4 us (4%)
  starting transfers between devices  11 us (3%)
  local copies, waits for them, and re-layouts  7.24 us (2%)
  matrix products  6.07 us (2%)
    psum x1, waiting for transfers between devices, per_device(): lax.psum((query_part, kernel_part), ('tm', 'rec'))  281 us
    all_gather x2, blocking collectives, merged(): everything = jax.tree.map(lambda part: lax.all_gather(part, axis), x)  24.1 us
    convert_element_type x1, other arithmetic, per_device(): jnp.where(is_valid[:, None], score_grad, 0.0).astype(jnp.bfloat16)  8.56 us
    ppermute x2, starting transfers between devices, with_halo(): before = lax.ppermute(last, axis, up)  8.38 us
    reduce_sum x4, other arithmetic, per_device(): jnp.sum(map_grad * padded[offset:offset + row_count], axis=0)  8.36 us
  transfers between devices with their start and end apart: 6, of which 3 were waited for; matrix products, arithmetic and copies ran while one was open for 3% of the time, Pallas kernels for 0%

commit v1 on v0

--- a/solution.py
+++ b/solution.py
@@ -93,7 +93,7 @@
             for offset in range(tap_count)
         ]
     )
-    query_whole, grad_kernel = lax.psum((query_part, kernel_part), ("tm", "rec"))
+    query_whole, grad_kernel = lax.psum(lax.psum((query_part, kernel_part), "tm"), "rec")
     col_count = width // lax.axis_size("rec")
     query_cols = lax.dynamic_slice_in_dim(
         query_whole, lax.axis_index("rec") * col_count, col_count, 1

time: 377 us -> 316 us (0.84)
  the two profiles are of different devices: /device:TPU:8 before, /device:TPU:1 now
where the time goes in v1:
time: 316 us
  waiting for transfers between devices  221 us (70%)
  blocking collectives  27.1 us (9%)
  other arithmetic  25.9 us (8%)
  between operations  16.4 us (5%)
  starting transfers between devices  11.1 us (4%)
  local copies, waits for them, and re-layouts  8.12 us (3%)
  matrix products  6.08 us (2%)
    psum x1, waiting for transfers between devices, per_device(): lax.psum((query_part, kernel_part), 'tm')  136 us
    psum x1, waiting for transfers between devices, per_device(): lax.psum(lax.psum((query_part, kernel_part), 'tm'), 'rec')  81.3 us
    all_gather x2, blocking collectives, merged(): everything = jax.tree.map(lambda part: lax.all_gather(part, axis), x)  27.1 us
    convert_element_type x1, other arithmetic, per_device(): jnp.where(is_valid[:, None], score_grad, 0.0).astype(jnp.bfloat16)  8.56 us
    reduce_sum x4, other arithmetic, per_device(): jnp.sum(map_grad * padded[offset:offset + row_count], axis=0)  8.36 us
    ppermute x2, starting transfers between devices, with_halo(): before = lax.ppermute(last, axis, up)  8.36 us
  transfers between devices with their start and end apart: 7, of which 3 were waited for; matrix products, arithmetic and copies ran while one was open for 4% of the time, Pallas kernels for 0%

profile of v1, /device:TPU:1, one launch (start us, length us, event | category | flops | bytes accessed | tf_op | source)
XLA Modules:
  0.0 315.8 jit_solution(17812967029710396932)
XLA Ops:
  8.0 0.0 all-reduce.5.cloned.1.call-start
  8.8 0.4 copy-done
  9.2 2.0 fusion
  11.3 4.4 %collective-permute-start = (f32[16,512]{1,0:T(8,128)S(1)}, f32[16,512]{1,0:T(8,128)S(1)}, u32[]{:S(2)}, u32[]{:S(2)}) collective-permute-start(f32[16,512]{1,0:T(8,128)S(1)} %get-tuple-element.194), channel_id=1, source_target_pairs={{0,32},{32,64},{64,96},{96,128},{128,160},{160,192},{192,224},{224... | collective-permute-start | bytes 98312 | tf_op jit(solution)/shard_map/ppermute | solution.py:25
  15.7 1.3 collective-permute-start.1
  17.1 3.4 %collective-permute-done.1 = f32[16,512]{1,0:T(8,128)S(1)} collective-permute-done((f32[16,512]{1,0:T(8,128)S(1)}, f32[16,512]{1,0:T(8,128)S(1)}, u32[]{:S(2)}, u32[]{:S(2)}) %collective-permute-start.1) | collective-permute-done | bytes 32800 | tf_op jit(solution)/shard_map/ppermute | solution.py:26
  20.5 5.1 %fusion.131 = (f32[512]{0:T(512)S(1)}, f32[512,512]{1,0:T(8,128)S(1)}) fusion(f32[16,512]{1,0:T(8,128)S(1)} %collective-permute-done.1, f32[512,512]{1,0:T(8,128)S(1)} %fusion, f32[512]{0:T(512)S(1)} %bitcast.126, f32[512]{0:T(512)S(1)} %bitcast.128, f32[512]{0:T(512)S(1)} %bitcast.132, f32[512]{0:T(512)S(1)} %bitcast.134, f32[512]{0:T(512)S(1)} %bitcast.136, ...), kind=kLoop, calls=%fused_computation.265 | loop fusion | flops 25689600 | bytes 2232320 | tf_op jit(solution)/shard_map/reduce_max | solution.py:49
  25.6 1.0 copy-done.1
  26.6 0.3 exponential_reduce_fusion
  26.9 15.8 %all-gather.3 = f32[8,1,512]{2,1,0:T(1,128)S(1)} all-gather(f32[1,1,512]{2,1,0:T(1,128)S(1)} %bitcast.194), channel_id=3, replica_groups=mesh['tm'=16,'query'=8,'rec'=4] {'query'}, dimensions={0}, use_global_device_ids=true | all-gather | bytes 18432 | tf_op jit(solution)/shard_map/all_gather | solution.py:9
  42.7 11.3 %all-gather.2 = f32[8,1,512]{2,1,0:T(1,128)S(1)} all-gather(f32[1,1,512]{2,1,0:T(1,128)S(1)} %bitcast.168), channel_id=2, replica_groups=mesh['tm'=16,'query'=8,'rec'=4] {'query'}, dimensions={0}, use_global_device_ids=true | all-gather | bytes 18432 | tf_op jit(solution)/shard_map/all_gather | solution.py:9
  54.0 0.4 while.17
  54.4 4.3 %multiply_reduce_fusion = (f32[512]{0:T(512)S(1)}, f32[512]{0:T(512)S(1)}, f32[512]{0:T(512)S(1)}, f32[512]{0:T(512)S(1)}, f32[512]{0:T(512)S(1)}, /*index=5*/f3...) fusion(f32[16,512]{1,0:T(8,128)S(1)} %collective-permute-done.1, ...), kind=kLoop, calls=%fused_computation.222 | loop fusion | flops 8646144 | bytes 3205632 | tf_op jit(solution)/shard_map/reduce_sum | solution.py:92
  58.7 1.3 collective-permute-start.2
  60.0 4.0 %collective-permute-start.3 = (f32[16,512]{1,0:T(8,128)S(1)}, f32[16,512]{1,0:T(8,128)S(1)}, u32[]{:S(2)}, u32[]{:S(2)}) collective-permute-start(f32[16,512]{1,0:T(8,128)S(1)} %get-tuple-element.193), channel_id=1, source_target_pairs={{0,32},{32,64},{64,96},{96,128},{128,160},{160,192},{192,224},{224... | collective-permute-start | bytes 98312 | tf_op jit(solution)/shard_map/ppermute | solution.py:25
  64.0 1.9 multiply_reduce_fusion.1
  65.9 1.2 multiply_reduce_fusion.17
  67.1 1.0 multiply_reduce_fusion.26
  68.1 3.9 %stack.135 = f32[33,512]{1,0:T(8,128)} concatenate(f32[1,512]{1,0:T(1,128)S(1)} %bitcast.193, f32[1,512]{1,0:T(1,128)S(1)} %bitcast.192, f32[1,512]{1,0:T(1,128)S(1)} %bitcast.191, f32[1,512]{1,0:T(1,128)S(1)} %bitcast.190, f32[1,512]{1,0:T(1,128)S(1)} %bitcast.189, f32[1,512]{1,0:T(1,128)S(1)} %bitcast.188, f32[1,512]{1,0:T(1,128)S(1)} %bitcast.187, f32[1,512]{1,0:T(1,128)S(1)} %bitcast.186, ...), dimensions={0} | concatenate | bytes 135168 | tf_op jit(solution)/shard_map/stack | solution.py:90
  72.0 8.6 %fusion.6 = bf16[512,512]{1,0:T(8,128)(2,1)S(1)} fusion(f32[16,512]{1,0:T(8,128)S(1)} %collective-permute-done.3, f32[16,512]{1,0:T(8,128)S(1)} %collective-permute-done.2, f32[512,512]{1,0:T(8,128)S(1)} %get-tuple-element.187, f32[512]{0:T(512)S(1)} %bitcast.127, f32[512]{0:T(512)S(1)} %bitcast.129, f32[512]{0:T(512)S(1)} %bitcast.133, ...), kind=kLoop, calls=%fused_computation.70 | loop fusion | flops 25952256 | bytes 1706496 | tf_op jit(solution)/shard_map/convert_element_type | solution.py:83
  80.6 2.0 fusion.127
  82.6 0.0 reduce-scatter.2.cloned.1.call-start
  82.7 1.1 copy-done.2
  83.8 2.0 fusion.136
  85.9 0.0 reduce-scatter.2.cloned.1.call-update
  85.9 0.0 all-reduce.7.cloned.1.call-start
  85.9 136.1 %all-reduce.5.cloned.1.call-done = (f32[512,1024]{1,0:T(8,128)}, f32[33,512]{1,0:T(8,128)}) async-done(((f32[512,1024]{1,0:T(8,128)}, f32[33,512]{1,0:T(8,128)}), (f32[512,1024]{1,0:T(8,128)}, f32[33,512]{1,0:T(8,128)})) %all-reduce.5.cloned.1.call-update) | async-done | bytes 2164752 | tf_op jit(solution)/shard_map/psum | solution.py:96
  222.0 0.0 reduce-scatter.2.cloned.1.call-done
  222.1 1.6 fusion.130
  223.7 81.3 %all-reduce.7.cloned.1.call-done = (f32[512,1024]{1,0:T(8,128)}, f32[33,512]{1,0:T(8,128)}) async-done(((f32[512,1024]{1,0:T(8,128)}, f32[33,512]{1,0:T(8,128)}), (f32[512,1024]{1,0:T(8,128)}, f32[33,512]{1,0:T(8,128)})) %all-reduce.7.cloned.1.call-update) | async-done | bytes 2164752 | tf_op jit(solution)/shard_map/psum | solution.py:96
  305.0 1.8 multiply_convert_fusion
  306.8 1.5 copy.28
  (38 shorter events, 0.4 us)
Async XLA Ops:
  8.0 1.2 copy-start
  8.0 214.0 %all-reduce.5.cloned.1.call-start = ((), (), s32[]{:S(2)}) async-start(), calls=%async_computation.2 | async-start | bytes 4358144 | tf_op jit(solution)/shard_map/psum | solution.py:96
  9.2 45.2 %copy-start.4 = (pred[512]{0:T(512)(128)(4,1)}, pred[512]{0:T(512)(128)(4,1)S(1)}, u32[]{:S(2)}) copy-start(pred[512]{0:T(512)(128)(4,1)S(1)} %add_compare_fusion) | copy-start | bytes 1540
  9.2 7.7 %copy-start.3 = (f32[33,512]{1,0:T(8,128)S(1)}, f32[33,512]{1,0:T(8,128)}, u32[]{:S(2)}) copy-start(f32[33,512]{1,0:T(8,128)} %param.9) | copy-start | bytes 202756
  11.3 5.8 %collective-permute-start = (f32[16,512]{1,0:T(8,128)S(1)}, f32[16,512]{1,0:T(8,128)S(1)}, u32[]{:S(2)}, u32[]{:S(2)}) collective-permute-start(f32[16,512]{1,0:T(8,128)S(1)} %get-tuple-element.194), channel_id=1, source_target_pairs={{0,32},{32,64},{64,96},{96,128},{128,160},{160,192},{192,224},{224... | collective-permute-start | bytes 98312 | tf_op jit(solution)/shard_map/ppermute | solution.py:25
  15.7 4.8 %collective-permute-start.1 = (f32[16,512]{1,0:T(8,128)S(1)}, f32[16,512]{1,0:T(8,128)S(1)}, u32[]{:S(2)}, u32[]{:S(2)}) collective-permute-start(f32[16,512]{1,0:T(8,128)S(1)} %get-tuple-element.195), channel_id=1, source_target_pairs={{32,0},{64,32},{96,64},{128,96},{160,128},{192,160},{224,192},{256... | collective-permute-start | bytes 98312 | tf_op jit(solution)/shard_map/ppermute | solution.py:26
  25.6 1.0 copy-start.1
  25.6 28.8 %copy-start.5 = (s32[1,512]{1,0:T(1,128)S(1)}, s32[1,512]{1,0:T(1,128)}, u32[]{:S(2)}) copy-start(s32[1,512]{1,0:T(1,128)} %param.10) | copy-start | bytes 6148
  58.7 13.3 %collective-permute-start.2 = (f32[16,512]{1,0:T(8,128)S(1)}, f32[16,512]{1,0:T(8,128)S(1)}, u32[]{:S(2)}, u32[]{:S(2)}) collective-permute-start(f32[16,512]{1,0:T(8,128)S(1)} %get-tuple-element.192), channel_id=1, source_target_pairs={{32,0},{64,32},{96,64},{128,96},{160,128},{192,160},{224,192},{256... | collective-permute-start | bytes 98312 | tf_op jit(solution)/shard_map/ppermute | solution.py:26
  60.0 12.0 %collective-permute-start.3 = (f32[16,512]{1,0:T(8,128)S(1)}, f32[16,512]{1,0:T(8,128)S(1)}, u32[]{:S(2)}, u32[]{:S(2)}) collective-permute-start(f32[16,512]{1,0:T(8,128)S(1)} %get-tuple-element.193), channel_id=1, source_target_pairs={{0,32},{32,64},{64,96},{96,128},{128,160},{160,192},{192,224},{224... | collective-permute-start | bytes 98312 | tf_op jit(solution)/shard_map/ppermute | solution.py:25
  82.6 1.2 copy-start.2
  82.6 139.4 %reduce-scatter.2.cloned.1.call-start = ((), (), s32[]{:S(2)}) async-start(), calls=%async_computation.1 | async-start | bytes 2359296 | tf_op jit(solution)/shard_map/reduce_scatter | solution.py:85
  85.9 219.1 %all-reduce.7.cloned.1.call-start = ((), (), s32[]{:S(2)}) async-start(), calls=%async_computation.3 | async-start | bytes 4358144 | tf_op jit(solution)/shard_map/psum | solution.py:96
Sparse Core Ops, SparseCore 0:
  82.7 139.2 all-reduce.4
  224.6 80.4 all-reduce.6
Sparse Core Ops, SparseCore 1:
  86.0 42.6 reduce-scatter.1
